TPU v7x, 32 devices: a whole 2x2x4 slice. The times are simulated.
32 devices in a mesh: row: 4 (over x, core), col: 8 (over z, y).
Axes of the slice: x: 2, y: 2, z: 4, core: 2. Of those that a mesh axis runs over, the one named last changes fastest.
Arguments:
- orbitals: bfloat16 [128, 16384], P(('row', 'col')), may hold values from -0.15722656 to 0.15722656
- gradient: bfloat16 [128, 16384], P(('row', 'col')), may hold values from -6 to 6
- stored: float32 [16384, 16384], P('row', 'col'), as said below
Outputs:
- projected: bfloat16 [128, 16384], P(('row', 'col'))
Inputs may be any that keep to these rules, and one draw needn't show every extreme that they name: stored is exactly symmetric: stored[i, j] equals stored[j, i].
All inputs are finite; a program needn't handle non-finite values.
Results may differ from a plain program's by a relative error of at most 0.0034.
Values may be sent and summed in bfloat16 or wider, within the bound.
A program may use at most 64 MiB of HBM per device.

v0:
```python
import jax
import jax.numpy as jnp
from jax import lax
from jax.sharding import PartitionSpec as P


def reorder(panel, outer, inner):
    width = panel.shape[1]
    shaped = panel.reshape(outer, inner, -1, width)
    return jnp.swapaxes(shaped, 0, 1).reshape(-1, width)


def inner_product(left, right):
    return lax.dot_general(
        left, right, (((0,), (0,)), ((), ())), preferred_element_type=jnp.float32
    )


def body(orbitals, gradient, stored):
    n_row = lax.axis_size("row")
    n_col = lax.axis_size("col")
    orb_q, grad_q = (
        lax.all_to_all(orbitals, "row", split_axis=1, concat_axis=0, tiled=True),
        lax.all_to_all(gradient, "row", split_axis=1, concat_axis=0, tiled=True),
    )
    orb_q, grad_q = (
        lax.all_gather(orb_q, "col", axis=0, tiled=True),
        lax.all_gather(grad_q, "col", axis=0, tiled=True),
    )
    orb_q = reorder(orb_q, n_col, n_row)
    grad_q = reorder(grad_q, n_col, n_row)
    orb_o, grad_o = (
        lax.all_to_all(orbitals, "col", split_axis=1, concat_axis=0, tiled=True),
        lax.all_to_all(gradient, "col", split_axis=1, concat_axis=0, tiled=True),
    )
    orb_o, grad_o = (
        lax.all_gather(orb_o, "row", axis=0, tiled=True),
        lax.all_gather(grad_o, "row", axis=0, tiled=True),
    )
    half = (0.5 * inner_product(orb_q, grad_o) + 0.5 * stored).astype(jnp.bfloat16)
    half_mirror = (0.5 * inner_product(grad_q, orb_o) + 0.5 * stored).astype(jnp.bfloat16)
    share = lax.psum_scatter(
        jnp.dot(orb_q, half, preferred_element_type=jnp.float32)
        + jnp.dot(orb_q, half_mirror, preferred_element_type=jnp.float32),
        "row",
        scatter_dimension=0,
        tiled=True,
    )
    correction = lax.all_to_all(share, "col", split_axis=0, concat_axis=1, tiled=True)
    return (gradient.astype(jnp.float32) - correction).astype(jnp.bfloat16)


def solution(mesh):
    return jax.shard_map(
        body,
        mesh=mesh,
        in_specs=(P(("row", "col"), None), P(("row", "col"), None), P("row", "col")),
        out_specs=P(("row", "col"), None),
        check_vma=False,
    )
```

profile of v0, /device:TPU:0, one launch (start us, length us, event | category | flops | bytes accessed | tf_op | source)
XLA Modules:
  0.0 187.5 jit_solution(17332358647925302149)
XLA Ops:
  6.5 8.8 %all_to_all.95 = bf16[4,4,4096]{2,0,1:T(4,128)(2,1)S(1)} all-to-all(bf16[4,4,4096]{2,0,1:T(4,128)(2,1)} %bitcast.28), channel_id=1, replica_groups=mesh['row'=4,'col'=8] {'row'}, dimensions={1} | all-to-all | bytes 262144 | tf_op jit(solution)/shard_map/all_to_all | solution.py:24
  15.4 0.7 all_to_all.81
  16.1 7.9 %all_to_all.96 = bf16[4,4,4096]{2,0,1:T(4,128)(2,1)S(1)} all-to-all(bf16[4,4,4096]{2,0,1:T(4,128)(2,1)} %bitcast.31), channel_id=1, replica_groups=mesh['row'=4,'col'=8] {'row'}, dimensions={1} | all-to-all | bytes 262144 | tf_op jit(solution)/shard_map/all_to_all | solution.py:23
  24.1 0.7 all_to_all.73
  24.8 14.1 %all_to_all.97 = bf16[4,8,2048]{2,0,1:T(4,128)(2,1)S(1)} all-to-all(bf16[4,8,2048]{2,0,1:T(4,128)(2,1)} %bitcast.29), channel_id=1, replica_groups=mesh['row'=4,'col'=8] {'col'}, dimensions={1} | all-to-all | bytes 262144 | tf_op jit(solution)/shard_map/all_to_all | solution.py:34
  38.9 3.4 %all-to-all-start.3 = ((bf16[4,8,2048]{2,0,1:T(4,128)(2,1)}), bf16[4,8,2048]{2,0,1:T(4,128)(2,1)S(1)}, u32[]{:S(2)}, u32[]{:S(2)}) async-start(bf16[4,8,2048]{2,0,1:T(4,128)(2,1)} %bitcast.32), calls=%async_computation.3 | async-start | bytes 262144 | tf_op jit(solution)/shard_map/all_to_all | solution.py:33
  42.2 0.0 reduce-scatter.4.cloned.1.call-start
  42.3 9.1 %all-to-all-done.3 = bf16[4,8,2048]{2,0,1:T(4,128)(2,1)S(1)} async-done(((bf16[4,8,2048]{2,0,1:T(4,128)(2,1)}), bf16[4,8,2048]{2,0,1:T(4,128)(2,1)S(1)}, u32[]{:S(2)}, u32[]{:S(2)}) %all-to-all-start.3) | async-done | bytes 131104 | tf_op jit(solution)/shard_map/all_to_all | solution.py:33
  51.5 7.1 %all_gather.15 = bf16[128,2048]{1,0:T(8,128)(2,1)} all-gather(bf16[32,2048]{1,0:T(8,128)(2,1)S(1)} %all_to_all.85), channel_id=1, replica_groups=mesh['row'=4,'col'=8] {'row'}, dimensions={0}, use_global_device_ids=true | all-gather | bytes 655360 | tf_op jit(solution)/shard_map/all_gather | solution.py:37
  58.5 7.7 %all_gather.13 = bf16[128,2048]{1,0:T(8,128)(2,1)} all-gather(bf16[32,2048]{1,0:T(8,128)(2,1)S(1)} %all_to_all.77), channel_id=1, replica_groups=mesh['row'=4,'col'=8] {'row'}, dimensions={0}, use_global_device_ids=true | all-gather | bytes 655360 | tf_op jit(solution)/shard_map/all_gather | solution.py:38
  66.2 1.5 reshape.29
  67.7 0.6 copy.23
  68.3 0.3 reshape.30
  68.6 32.1 %all-gather.3.cloned.1.call-done = bf16[128,4096]{1,0:T(8,128)(2,1)} async-done(((bf16[16,4096]{1,0:T(8,128)(2,1)}), bf16[128,4096]{1,0:T(8,128)(2,1)}) %all-gather.3.cloned.1.call-update) | async-done | bytes 1048592 | tf_op jit(solution)/shard_map/all_gather | solution.py:27
  100.7 1.5 reshape.27
  102.1 0.6 copy.24
  102.8 0.3 reshape.28
  103.1 22.3 %fusion = f32[2048,128]{1,0:T(8,128)} fusion(bf16[128,4096]{1,0:T(8,128)(2,1)S(1)} %reshape.28, f32[4096,2048]{1,0:T(8,128)} %param.5, bf16[128,2048]{1,0:T(8,128)(2,1)} %all_gather.13), kind=kOutput, calls=%fused_computation.2 | convolution fusion | flops 4328521728 | bytes 36175872 | tf_op jit(solution)/shard_map/dot_general | solution.py:43
  125.3 14.5 %fusion.7 = f32[128,2048]{0,1:T(8,128)S(1)} fusion(f32[2048,128]{1,0:T(8,128)} %fusion, bf16[128,4096]{1,0:T(8,128)(2,1)S(1)} %reshape.28, f32[4096,2048]{1,0:T(8,128)} %param.5, bf16[128,4096]{1,0:T(8,128)(2,1)S(1)} %reshape.30, bf16[128,2048]{1,0:T(8,128)(2,1)} %all_gather.15), kind=kOutput, calls=%fused_computation.7 | convolution fusion | flops 4328783872 | bytes 38273024 | tf_op jit(solution)/shard_map/dot_general | solution.py:44
  139.9 1.3 copy.19
  141.2 23.8 %reduce-scatter.4.cloned.1.call-done = f32[32,2048]{1,0:T(8,128)} async-done(((f32[128,2048]{1,0:T(8,128)}), f32[32,2048]{1,0:T(8,128)}) %reduce-scatter.4.cloned.1.call-update) | async-done | bytes 262160 | tf_op jit(solution)/shard_map/reduce_scatter | solution.py:42
  165.0 1.0 all_to_all.86
  166.0 14.2 %all_to_all.98 = f32[8,4,2048]{2,1,0:T(4,128)S(1)} all-to-all(f32[8,4,2048]{2,1,0:T(4,128)S(1)} %all_to_all.86), channel_id=1, replica_groups=mesh['row'=4,'col'=8] {'col'}, dimensions={0} | all-to-all | bytes 524288 | tf_op jit(solution)/shard_map/all_to_all | solution.py:49
  180.2 0.7 subtract_convert_fusion
  (10 shorter events, 0.2 us)
Async XLA Ops:
  6.5 59.7 %all-gather.5.cloned.1.call-start = ((), (), s32[]{:S(2)}) async-start(), calls=%async_computation.7 | async-start | bytes 1179648 | tf_op jit(solution)/shard_map/all_gather | solution.py:28
  16.1 84.6 %all-gather.3.cloned.1.call-start = ((), (), s32[]{:S(2)}) async-start(), calls=%async_computation.6 | async-start | bytes 1179648 | tf_op jit(solution)/shard_map/all_gather | solution.py:27
  38.9 12.6 %all-to-all-start.3 = ((bf16[4,8,2048]{2,0,1:T(4,128)(2,1)}), bf16[4,8,2048]{2,0,1:T(4,128)(2,1)S(1)}, u32[]{:S(2)}, u32[]{:S(2)}) async-start(bf16[4,8,2048]{2,0,1:T(4,128)(2,1)} %bitcast.32), calls=%async_computation.3 | async-start | bytes 262144 | tf_op jit(solution)/shard_map/all_to_all | solution.py:33
  42.2 122.8 %reduce-scatter.4.cloned.1.call-start = ((), (), s32[]{:S(2)}) async-start(), calls=%async_computation.8 | async-start | bytes 1310720 | tf_op jit(solution)/shard_map/reduce_scatter | solution.py:42
  125.3 54.9 %copy-start = (bf16[4,16384]{1,0:T(4,128)(2,1)S(1)}, bf16[4,16384]{1,0:T(4,128)(2,1)}, u32[]{:S(2)}) copy-start(bf16[4,16384]{1,0:T(4,128)(2,1)} %param.4) | copy-start | bytes 393220
Sparse Core Ops, SparseCore 0:
  16.2 43.4 all-gather.4
  61.9 38.7 all-gather.2
  141.3 23.6 reduce-scatter.3
where the time goes:
time: 188 us; the launch traced here: 187 us
  waiting for transfers between devices  65 us (35%)
  blocking collectives  59.9 us (32%)
  matrix products  36.8 us (20%)
  between operations  13.2 us (7%)
  local copies, waits for them, and re-layouts  8.48 us (5%)
  starting transfers between devices  3.46 us (2%)
    all_gather x1, waiting for transfers between devices, body(): lax.all_gather(orb_q, 'col', axis=0, tiled=True)  32.1 us
    reduce_scatter x1, waiting for transfers between devices, body(): lax.psum_scatter(jnp.dot(orb_q, half, preferred_element_type=jnp.float32)...  23.8 us
    dot_general x1, matrix products, body(): jnp.dot(orb_q, half, preferred_element_type=jnp.float32)  22.3 us
    dot_general x1, matrix products, body(): jnp.dot(orb_q, half_mirror, preferred_element_type=jnp.float32)  14.5 us
    all_to_all x1, blocking collectives, body(): lax.all_to_all(share, 'col', split_axis=0, concat_axis=1, tiled=True)  14.2 us
    all_to_all x1, blocking collectives, body(): lax.all_to_all(gradient, 'col', split_axis=1, concat_axis=0, tiled=True)  14.1 us
    all_to_all x1, waiting for transfers between devices, body(): lax.all_to_all(orbitals, 'col', split_axis=1, concat_axis=0, tiled=True)  9.09 us
    all_to_all x1, blocking collectives, body(): lax.all_to_all(gradient, 'row', split_axis=1, concat_axis=0, tiled=True)  8.84 us
  transfers between devices with their start and end apart: 4, of which 3 were waited for; matrix products, arithmetic and copies ran while one was open for 1% of the time, Pallas kernels for 0%

commit v1 on v0

--- a/solution.py
+++ b/solution.py
@@ -1,7 +1,17 @@
+import functools
+
 import jax
 import jax.numpy as jnp
 from jax import lax
+from jax.experimental import pallas as pl
+from jax.experimental.pallas import tpu as pltpu
 from jax.sharding import PartitionSpec as P
+
+MESH = pl.DeviceIdType.MESH
+LANES = 128
+TILE = 16
+CHUNKS = 4
+S_COPIES = 8
 
 
 def reorder(panel, outer, inner):
@@ -16,7 +26,11 @@
     )
 
 
-def body(orbitals, gradient, stored):
+def dot(left, right):
+    return jnp.dot(left, right, preferred_element_type=jnp.float32)
+
+
+def general_body(orbitals, gradient, stored):
     n_row = lax.axis_size("row")
     n_col = lax.axis_size("col")
     orb_q, grad_q = (
@@ -40,14 +54,322 @@
     half = (0.5 * inner_product(orb_q, grad_o) + 0.5 * stored).astype(jnp.bfloat16)
     half_mirror = (0.5 * inner_product(grad_q, orb_o) + 0.5 * stored).astype(jnp.bfloat16)
     share = lax.psum_scatter(
-        jnp.dot(orb_q, half, preferred_element_type=jnp.float32)
-        + jnp.dot(orb_q, half_mirror, preferred_element_type=jnp.float32),
-        "row",
-        scatter_dimension=0,
-        tiled=True,
+        dot(orb_q, half) + dot(orb_q, half_mirror), "row", scatter_dimension=0, tiled=True
     )
     correction = lax.all_to_all(share, "col", split_axis=0, concat_axis=1, tiled=True)
     return (gradient.astype(jnp.float32) - correction).astype(jnp.bfloat16)
+
+
+def kernel(
+    n_row, n_col, own, width,
+    xg, s_hbm, out,
+    sbuf, rowbuf, xq, gsh, acc, rbuf, xout, xbuf, ebuf, xe, ge, perm, cbuf, ab, fbuf,
+    s_sem, row_send, row_recv, e_send, e_recv, g_send, g_recv,
+    c_send, c_recv, ab_send, ab_recv, core_send, core_recv, x_send, x_recv, f_send, f_recv,
+):
+    n_dev = n_row * n_col
+    n_z = n_col // 2
+    groups = width // LANES
+    part = n_col // CHUNKS
+    deep = part * width
+    r, c = lax.axis_index("row"), lax.axis_index("col")
+    me = c * n_row + r
+    z, y = lax.div(c, 2), lax.rem(c, 2)
+    core, chip = lax.rem(r, 2), lax.div(r, 2)
+    near = chip * 2 + 1 - core
+    far = (1 - chip) * 2 + core
+    cross = (1 - chip) * 2 + 1 - core
+
+    def device(d):
+        return {"row": lax.rem(d, n_row), "col": lax.div(d, n_row)}
+
+    def remote(src, dst, send, recv, target):
+        return pltpu.make_async_remote_copy(
+            src_ref=src, dst_ref=dst, send_sem=send, recv_sem=recv,
+            device_id=target, device_id_type=MESH,
+        )
+
+    depth = sbuf.shape[0] // S_COPIES
+
+    def s_copy(i):
+        rows = pl.ds(i * depth, depth)
+        return pltpu.make_async_copy(s_hbm.at[rows, :], sbuf.at[rows, :], s_sem.at[i])
+
+    def others(count, mine, body):
+        @pl.loop(1, count)
+        def _(i):
+            body(lax.rem(mine + i, count))
+
+    barrier = pltpu.get_barrier_semaphore()
+    others(n_dev, me, lambda d: pl.semaphore_signal(
+        barrier, inc=1, device_id=device(d), device_id_type=MESH))
+    for i in range(S_COPIES):
+        s_copy(i).start()
+    pl.semaphore_wait(barrier, n_dev - 1)
+
+    def row_copy(p, q):
+        return remote(
+            xg.at[pl.ds(p * n_col, n_col)], rowbuf.at[q],
+            row_send.at[p], row_recv.at[q], {"row": p, "col": c},
+        )
+
+    others(n_row, r, lambda p: row_copy(p, r).start())
+    rowbuf[r] = xg[pl.ds(r * n_col, n_col)]
+
+    def e_copy(d, s):
+        return remote(xg.at[d], ebuf.at[s], e_send.at[d], e_recv.at[s], device(d))
+
+    n_out = n_dev * TILE
+    at = lax.broadcasted_iota(jnp.int32, (n_out, n_out), 0)
+    of = lax.broadcasted_iota(jnp.int32, (n_out, n_out), 1)
+    wide = n_dev * own
+    tile_row = lax.div(lax.rem(at, wide), own) * TILE + lax.div(at, wide) * own + lax.rem(at, own)
+    perm[...] = jnp.where(tile_row == of, 1.0, 0.0).astype(jnp.bfloat16)
+    at = lax.broadcasted_iota(jnp.int32, (n_row * TILE, n_row * TILE), 0)
+    of = lax.broadcasted_iota(jnp.int32, (n_row * TILE, n_row * TILE), 1)
+    tall = n_row * own
+    small_row = lax.div(lax.rem(at, tall), own) * TILE + lax.div(at, tall) * own + lax.rem(at, own)
+    small = jnp.where(small_row == of, 1.0, 0.0).astype(jnp.bfloat16)
+
+    others(n_row, r, lambda q: row_copy(q, q).wait_recv())
+
+    def shard(k, o):
+        return xq.at[k, pl.ds(pl.multiple_of(o * tall, tall), tall), :]
+
+    def g_copy(k, o, way):
+        target = (c + 2, c - 2, z * 2 + 1 - y)[way]
+        return remote(
+            shard(k, o), shard(k, o), g_send.at[k, o, way], g_recv.at[k, o],
+            {"row": r, "col": target},
+        )
+
+    def pass_on(k, o, do, up, down):
+        if up:
+            pl.when(z < n_z - 1)(lambda: do(g_copy(k, o, 0)))
+        if down:
+            pl.when(z > 0)(lambda: do(g_copy(k, o, 1)))
+        do(g_copy(k, o, 2))
+
+    def start(copy):
+        copy.start()
+
+    def wait_send(copy):
+        copy.wait_send()
+
+    def post(k):
+        mine = pl.ds(pl.multiple_of(c * tall, tall), tall)
+        for b in range(part):
+            for t in range(2):
+                block = rowbuf[:, k * part + b, t].reshape(n_row * TILE, LANES)
+                turned = dot(small, block).astype(jnp.bfloat16)
+                for g in range(groups):
+                    piece = turned[g * tall:(g + 1) * tall]
+                    lanes = pl.ds(b * width + g * LANES, LANES)
+                    gsh[k, t * tall:(t + 1) * tall, lanes] = piece
+                    if t == 0:
+                        xq[k, mine, lanes] = piece
+        pass_on(k, c, start, True, True)
+
+    def forward(k, d):
+        @pl.when(z >= d)
+        def _():
+            o = c - 2 * d
+            g_copy(k, o, 2).wait_recv()
+            pass_on(k, o, start, True, False)
+
+        @pl.when(z + d < n_z)
+        def _():
+            o = c + 2 * d
+            g_copy(k, o, 2).wait_recv()
+            pass_on(k, o, start, False, True)
+
+    def blocks_product(k, j):
+        rows = pl.ds(k * deep, deep)
+        cols = pl.ds(pl.multiple_of(j * width, width), width)
+        return dot(xq[k], sbuf[rows, cols].astype(jnp.bfloat16))
+
+    def inner(k):
+        return lax.dot_general(
+            gsh[k], xq[k], (((1,), (1,)), ((), ())), preferred_element_type=jnp.float32)
+
+    def complete(k):
+        for z0 in range(n_z):
+            g_copy(k, z0 * 2 + 1 - y, 2).wait_recv()
+        for i in range(k * S_COPIES // CHUNKS, (k + 1) * S_COPIES // CHUNKS):
+            s_copy(i).wait()
+
+    for k in range(CHUNKS):
+        post(k)
+    others(n_dev, me, lambda d: e_copy(d, me).start())
+    ebuf[me] = xg[me]
+
+    gram = None
+    for step in range(1, CHUNKS + n_z - 1):
+        for d in range(n_z - 1, 0, -1):
+            if 0 <= step - d < CHUNKS:
+                forward(step - d, d)
+        k = step - (n_z - 1)
+        if 0 <= k < CHUNKS - 1:
+            complete(k)
+            gram = inner(k) if gram is None else gram + inner(k)
+
+            @pl.loop(0, n_row)
+            def _(j, k=k):
+                if k == 0:
+                    acc[j] = blocks_product(k, j)
+                else:
+                    acc[j] += blocks_product(k, j)
+
+    last = CHUNKS - 1
+    complete(last)
+    cbuf[r] = gram + inner(last)
+
+    def c_copy(p, q):
+        return remote(cbuf.at[q], cbuf.at[q], c_send.at[p], c_recv.at[q], {"row": p, "col": c})
+
+    others(n_row, r, lambda p: c_copy(p, r).start())
+
+    def core_copy(i, j):
+        return remote(acc.at[j], rbuf.at[i], core_send.at[i], core_recv.at[i],
+                      {"row": near, "col": c})
+
+    acc[cross] += blocks_product(last, cross)
+    core_copy(0, cross).start()
+    acc[near] += blocks_product(last, near)
+    core_copy(1, near).start()
+
+    others(n_row, r, lambda q: c_copy(q, q).wait_recv())
+    total = cbuf[0]
+    for q in range(1, n_row):
+        total = total + cbuf[q]
+    ab[c] = total
+
+    def ab_copy(p, q):
+        return remote(ab.at[q], ab.at[q], ab_send.at[p], ab_recv.at[q], {"row": r, "col": p})
+
+    others(n_col, c, lambda p: ab_copy(p, c).start())
+
+    acc[far] += blocks_product(last, far)
+    core_copy(0, cross).wait_recv()
+    xout[...] = (acc[far] + rbuf[0]).astype(jnp.bfloat16)
+    x_copy = remote(xout, xbuf, x_send, x_recv, {"row": far, "col": c})
+    x_copy.start()
+    acc[r] += blocks_product(last, r)
+
+    others(n_dev, me, lambda s: e_copy(s, s).wait_recv())
+    for t, dest in ((0, xe), (1, ge)):
+        turned = dot(perm[...], ebuf[:, t].reshape(n_out, LANES)).astype(jnp.bfloat16)
+        for g in range(groups):
+            dest[:, g * LANES:(g + 1) * LANES] = turned[g * wide:(g + 1) * wide]
+
+    others(n_col, c, lambda q: ab_copy(q, q).wait_recv())
+    orb_orb = ab[:, :tall, :].reshape(wide, wide)
+    orb_grad = ab[:, tall:, :].reshape(wide, wide).T
+
+    def accurate(left, right):
+        high = left.astype(jnp.bfloat16)
+        low = (left - high.astype(jnp.float32)).astype(jnp.bfloat16)
+        return dot(high, right) + dot(low, right)
+
+    rest = ge[...].astype(jnp.float32) - 0.5 * (
+        accurate(orb_orb, ge[...]) + accurate(orb_grad, xe[...]))
+    core_copy(1, near).wait_recv()
+    rest = rest - (acc[r] + rbuf[1])
+    x_copy.wait_recv()
+    result = (rest - xbuf[...].astype(jnp.float32)).astype(jnp.bfloat16)
+    stack = jnp.concatenate([result[:, g * LANES:(g + 1) * LANES] for g in range(groups)], axis=0)
+    tiles = lax.dot_general(
+        perm[...], stack, (((0,), (0,)), ((), ())), preferred_element_type=jnp.float32)
+    fbuf[...] = tiles.astype(jnp.bfloat16).reshape(n_dev, TILE, LANES)
+
+    def f_copy(d, s):
+        return remote(fbuf.at[d], out.at[s], f_send.at[d], f_recv.at[s], device(d))
+
+    others(n_dev, me, lambda d: f_copy(d, me).start())
+    out[me] = fbuf[me]
+
+    others(n_row, r, lambda p: row_copy(p, r).wait_send())
+    others(n_row, r, lambda p: c_copy(p, r).wait_send())
+    others(n_col, c, lambda p: ab_copy(p, c).wait_send())
+    others(n_dev, me, lambda d: e_copy(d, me).wait_send())
+    for k in range(CHUNKS):
+        pass_on(k, c, wait_send, True, True)
+        for d in range(1, n_z):
+            pl.when(z >= d)(lambda k=k, d=d: pass_on(k, c - 2 * d, wait_send, True, False))
+            pl.when(z + d < n_z)(lambda k=k, d=d: pass_on(k, c + 2 * d, wait_send, False, True))
+    core_copy(0, cross).wait_send()
+    core_copy(1, near).wait_send()
+    x_copy.wait_send()
+    others(n_dev, me, lambda s: f_copy(s, s).wait_recv())
+    others(n_dev, me, lambda d: f_copy(d, me).wait_send())
+
+
+def kernel_body(n_row, n_col, orbitals, gradient, stored):
+    own, n_orb = orbitals.shape
+    n_dev = n_row * n_col
+    width = n_orb // n_dev
+    groups = width // LANES
+    n_pw = own * n_dev
+    tall = n_row * own
+    deep = n_orb // n_row // CHUNKS
+
+    def tiled(rows):
+        shaped = rows.reshape(own, n_dev, groups, LANES)
+        return shaped.transpose(1, 2, 0, 3).reshape(n_dev, 1, TILE, LANES)
+
+    xg = jnp.concatenate([tiled(orbitals), tiled(gradient)], axis=1)
+    bf16, f32 = jnp.bfloat16, jnp.float32
+    dma = pltpu.SemaphoreType.DMA
+    tiles = pl.pallas_call(
+        functools.partial(kernel, n_row, n_col, own, width),
+        out_shape=jax.ShapeDtypeStruct((n_dev, TILE, LANES), bf16),
+        in_specs=[pl.BlockSpec(memory_space=pltpu.VMEM), pl.BlockSpec(memory_space=pl.ANY)],
+        out_specs=pl.BlockSpec(memory_space=pltpu.VMEM),
+        scratch_shapes=[
+            pltpu.VMEM(stored.shape, f32),
+            pltpu.VMEM((n_row, n_col, 2, TILE, LANES), bf16),
+            pltpu.VMEM((CHUNKS, n_pw, deep), bf16),
+            pltpu.VMEM((CHUNKS, 2 * tall, deep), bf16),
+            pltpu.VMEM((n_row, n_pw, width), f32),
+            pltpu.VMEM((2, n_pw, width), f32),
+            pltpu.VMEM((n_pw, width), bf16),
+            pltpu.VMEM((n_pw, width), bf16),
+            pltpu.VMEM((n_dev, 2, TILE, LANES), bf16),
+            pltpu.VMEM((n_pw, width), bf16),
+            pltpu.VMEM((n_pw, width), bf16),
+            pltpu.VMEM((n_dev * TILE, n_dev * TILE), bf16),
+            pltpu.VMEM((n_row, 2 * tall, n_pw), f32),
+            pltpu.VMEM((n_col, 2 * tall, n_pw), f32),
+            pltpu.VMEM((n_dev, TILE, LANES), bf16),
+            dma((S_COPIES,)), dma((n_row,)), dma((n_row,)), dma((n_dev,)), dma((n_dev,)),
+            dma((CHUNKS, n_col, 3)), dma((CHUNKS, n_col)),
+            dma((n_row,)), dma((n_row,)), dma((n_col,)), dma((n_col,)),
+            dma((2,)), dma((2,)), dma(()), dma(()), dma((n_dev,)), dma((n_dev,)),
+        ],
+        compiler_params=pltpu.CompilerParams(
+            collective_id=0, has_side_effects=True, vmem_limit_bytes=56 * 1024 * 1024),
+        cost_estimate=pl.CostEstimate(
+            flops=2 * n_pw * stored.size, bytes_accessed=4 * stored.size, transcendentals=0),
+    )(xg, stored)
+    shaped = tiles.reshape(n_dev, groups, own, LANES)
+    return shaped.transpose(2, 0, 1, 3).reshape(own, n_orb)
+
+
+def body(orbitals, gradient, stored):
+    n_row = lax.axis_size("row")
+    n_col = lax.axis_size("col")
+    own, n_orb = orbitals.shape
+    n_dev = n_row * n_col
+    width = n_orb // n_dev
+    fits = (
+        n_row == 4 and n_col % CHUNKS == 0 and width % LANES == 0
+        and own * width == TILE * LANES and own * n_row == TILE
+        and own * n_dev == LANES and stored.shape[0] % S_COPIES == 0
+        and stored.size * 4 <= 32 * 1024 * 1024
+    )
+    if fits:
+        return kernel_body(n_row, n_col, orbitals, gradient, stored)
+    return general_body(orbitals, gradient, stored)
 
 
 def solution(mesh):

time: 188 us -> 62.3 us (0.33)
  waiting for transfers between devices: 65 us -> 0 us
  blocking collectives: 59.9 us -> 0 us
  Pallas kernels: 0 us -> 58.8 us
  matrix products: 36.8 us -> 0 us
  between operations: 13.2 us -> 0.01 us
  local copies, waits for them, and re-layouts: 8.48 us -> 1.61 us
  starting transfers between devices: 3.46 us -> 0 us
    pallas_call x0 -> x1, Pallas kernels: none -> 58.8 us  [kernel_body(): pl.pallas_call(functools.partial(kernel, n_row, n_col, own, width), out_s...]
    all_to_all x4 -> x0, blocking collectives: 45.1 us -> none  [the longest x1 14.2 us: body(): lax.all_to_all(share, 'col', split_axis=0, concat_axis=1, tiled=True)]
    dot_general x2 -> x0, matrix products: 36.8 us -> none  [the longest x1 22.3 us: body(): jnp.dot(orb_q, half, preferred_element_type=jnp.float32)]
    all_gather x2 -> x0, waiting for transfers between devices: 32.1 us -> none  [the longest x1 32.1 us: body(): lax.all_gather(orb_q, 'col', axis=0, tiled=True)]
    reduce_scatter x1 -> x0, waiting for transfers between devices: 23.8 us -> none  [body(): lax.psum_scatter(jnp.dot(orb_q, half, preferred_element_type=jnp.float32)...]
    all_gather x2 -> x0, blocking collectives: 14.8 us -> none  [the longest x1 7.73 us: body(): lax.all_gather(grad_o, 'row', axis=0, tiled=True)]
    all_to_all x1 -> x0, waiting for transfers between devices: 9.09 us -> none  [body(): lax.all_to_all(orbitals, 'col', split_axis=1, concat_axis=0, tiled=True)]
    reshape x6 -> x0, local copies, waits for them, and re-layouts: 4.71 us -> none  [the longest x4 4.15 us: reorder(): shaped = panel.reshape(outer, inner, -1, width)]
  transfers between devices with their start and end apart: 4 -> 0, of which waited for: 3 -> 0; matrix products, arithmetic and copies ran while one was open for 1% -> 0% of each run, Pallas kernels for 0% -> 0%
where the time goes in v1:
time: 62.3 us; the launch traced here: 62.1 us
  Pallas kernels  58.8 us (94%)
  other arithmetic  1.68 us (3%)
  local copies, waits for them, and re-layouts  1.61 us (3%)
    pallas_call x1, Pallas kernels, kernel_body(): pl.pallas_call(functools.partial(kernel, n_row, n_col, own, width), out_s...  58.8 us
    concatenate x1, other arithmetic, kernel_body(): xg = jnp.concatenate([tiled(orbitals), tiled(gradient)], axis=1)  1.68 us
    unnamed x1, local copies, waits for them, and re-layouts  1.61 us

profile of v1, /device:TPU:0, one launch (start us, length us, event | category | flops | bytes accessed | tf_op | source)
XLA Modules:
  0.0 62.1 jit_solution(4919822837724768116)
XLA Ops:
  0.0 1.7 %pad_maximum_fusion.xg = bf16[32,2,16,128]{3,2,1,0:T(8,128)(2,1)} fusion(bf16[32,1,16,128]{3,2,1,0:T(8,128)(2,1)} %bitcast.16, bf16[32,1,16,128]{3,2,1,0:T(8,128)(2,1)} %bitcast.17), kind=kLoop, calls=%fused_computation | loop fusion | flops 131072 | bytes 524288 | tf_op jit(solution)/shard_map/concatenate | solution.py:320
  1.7 58.8 %shard_map.37 = bf16[32,16,128]{2,1,0:T(8,128)(2,1)} custom-call(bf16[32,2,16,128]{3,2,1,0:T(8,128)(2,1)} %pad_maximum_fusion.xg, f32[4096,2048]{1,0:T(8,128)} %s_hbm.1), custom_call_target="tpu_custom_call" | custom-call | flops 2147483648 | bytes 33554432 | tf_op jit(solution)/shard_map/pallas_call | solution.py:323
  60.5 1.6 %copy.8 = bf16[4,16384]{1,0:T(4,128)(2,1)} copy(bf16[4,16384]{1,0:T(4,128)(2,1)} %bitcast.15) | data formatting | bytes 262144

commit v2 on v1

--- a/solution.py
+++ b/solution.py
@@ -2,6 +2,7 @@
 
 import jax
 import jax.numpy as jnp
+import numpy as np
 from jax import lax
 from jax.experimental import pallas as pl
 from jax.experimental.pallas import tpu as pltpu
@@ -12,6 +13,7 @@
 TILE = 16
 CHUNKS = 4
 S_COPIES = 8
+S_SLOTS = 6
 
 
 def reorder(panel, outer, inner):
@@ -62,9 +64,9 @@
 
 def kernel(
     n_row, n_col, own, width,
-    xg, s_hbm, out,
-    sbuf, rowbuf, xq, gsh, acc, rbuf, xout, xbuf, ebuf, xe, ge, perm, cbuf, ab, fbuf,
-    s_sem, row_send, row_recv, e_send, e_recv, g_send, g_recv,
+    x_hbm, g_hbm, perm_hbm, small_hbm, s_hbm, out,
+    xg, small, sbuf, sb, rowbuf, xq, gsh, acc, rbuf, xout, xbuf, ebuf, xe, ge, perm, cbuf, ab, fbuf,
+    in_sem, s_sem, row_send, row_recv, e_send, e_recv, g_send, g_recv,
     c_send, c_recv, ab_send, ab_recv, core_send, core_recv, x_send, x_recv, f_send, f_recv,
 ):
     n_dev = n_row * n_col
@@ -89,11 +91,38 @@
             device_id=target, device_id_type=MESH,
         )
 
-    depth = sbuf.shape[0] // S_COPIES
+    depth = sbuf.shape[1]
+    strip = 32
 
     def s_copy(i):
-        rows = pl.ds(i * depth, depth)
-        return pltpu.make_async_copy(s_hbm.at[rows, :], sbuf.at[rows, :], s_sem.at[i])
+        return pltpu.make_async_copy(
+            s_hbm.at[pl.ds(i * depth, depth), :], sbuf.at[i % S_SLOTS], s_sem.at[i])
+
+    def convert(i):
+        s_copy(i).wait()
+
+        @pl.loop(0, depth // strip)
+        def _(n):
+            rows = pl.ds(pl.multiple_of(n * strip, strip), strip)
+            into = pl.ds(pl.multiple_of(i * depth + n * strip, strip), strip)
+            sb[into, :] = sbuf[i % S_SLOTS, rows, :].astype(jnp.bfloat16)
+
+        if i + S_SLOTS < S_COPIES:
+            s_copy(i + S_SLOTS).start()
+
+    local = [
+        pltpu.make_async_copy(x_hbm, xg.at[:, 0], in_sem.at[0]),
+        pltpu.make_async_copy(g_hbm, xg.at[:, 1], in_sem.at[1]),
+        pltpu.make_async_copy(small_hbm, small, in_sem.at[2]),
+    ] + [
+        pltpu.make_async_copy(
+            perm_hbm.at[g], perm.at[:, pl.ds(g * LANES, LANES)], in_sem.at[3 + g])
+        for g in range(perm_hbm.shape[0])
+    ]
+    for copy in local:
+        copy.start()
+    for i in range(S_SLOTS):
+        s_copy(i).start()
 
     def others(count, mine, body):
         @pl.loop(1, count)
@@ -103,8 +132,8 @@
     barrier = pltpu.get_barrier_semaphore()
     others(n_dev, me, lambda d: pl.semaphore_signal(
         barrier, inc=1, device_id=device(d), device_id_type=MESH))
-    for i in range(S_COPIES):
-        s_copy(i).start()
+    for copy in local:
+        copy.wait()
     pl.semaphore_wait(barrier, n_dev - 1)
 
     def row_copy(p, q):
@@ -119,36 +148,34 @@
     def e_copy(d, s):
         return remote(xg.at[d], ebuf.at[s], e_send.at[d], e_recv.at[s], device(d))
 
+    others(n_dev, me, lambda d: e_copy(d, me).start())
+    ebuf[me] = xg[me]
     n_out = n_dev * TILE
-    at = lax.broadcasted_iota(jnp.int32, (n_out, n_out), 0)
-    of = lax.broadcasted_iota(jnp.int32, (n_out, n_out), 1)
     wide = n_dev * own
-    tile_row = lax.div(lax.rem(at, wide), own) * TILE + lax.div(at, wide) * own + lax.rem(at, own)
-    perm[...] = jnp.where(tile_row == of, 1.0, 0.0).astype(jnp.bfloat16)
-    at = lax.broadcasted_iota(jnp.int32, (n_row * TILE, n_row * TILE), 0)
-    of = lax.broadcasted_iota(jnp.int32, (n_row * TILE, n_row * TILE), 1)
     tall = n_row * own
-    small_row = lax.div(lax.rem(at, tall), own) * TILE + lax.div(at, tall) * own + lax.rem(at, own)
-    small = jnp.where(small_row == of, 1.0, 0.0).astype(jnp.bfloat16)
+    for i in range(S_COPIES // 2):
+        convert(i)
 
     others(n_row, r, lambda q: row_copy(q, q).wait_recv())
 
     def shard(k, o):
         return xq.at[k, pl.ds(pl.multiple_of(o * tall, tall), tall), :]
 
-    def g_copy(k, o, way):
-        target = (c + 2, c - 2, z * 2 + 1 - y)[way]
+    def g_copy(k, o, send, target):
         return remote(
-            shard(k, o), shard(k, o), g_send.at[k, o, way], g_recv.at[k, o],
-            {"row": r, "col": target},
-        )
-
-    def pass_on(k, o, do, up, down):
-        if up:
-            pl.when(z < n_z - 1)(lambda: do(g_copy(k, o, 0)))
-        if down:
-            pl.when(z > 0)(lambda: do(g_copy(k, o, 1)))
-        do(g_copy(k, o, 2))
+            shard(k, o), shard(k, o), send, g_recv.at[k, o], {"row": r, "col": target})
+
+    def along_z(k, side, d):
+        return g_copy(k, c, g_send.at[k, side, d, 0], c + 2 * d if side == 0 else c - 2 * d)
+
+    def along_y(k, side, d, o):
+        return g_copy(k, o, g_send.at[k, side, d, 1], z * 2 + 1 - y)
+
+    def spread(k, do):
+        do(along_y(k, 0, 0, c))
+        for d in range(1, n_z):
+            pl.when(z + d < n_z)(lambda d=d: do(along_z(k, 0, d)))
+            pl.when(z >= d)(lambda d=d: do(along_z(k, 1, d)))
 
     def start(copy):
         copy.start()
@@ -161,32 +188,30 @@
         for b in range(part):
             for t in range(2):
                 block = rowbuf[:, k * part + b, t].reshape(n_row * TILE, LANES)
-                turned = dot(small, block).astype(jnp.bfloat16)
+                turned = dot(small[...], block).astype(jnp.bfloat16)
                 for g in range(groups):
                     piece = turned[g * tall:(g + 1) * tall]
                     lanes = pl.ds(b * width + g * LANES, LANES)
                     gsh[k, t * tall:(t + 1) * tall, lanes] = piece
                     if t == 0:
                         xq[k, mine, lanes] = piece
-        pass_on(k, c, start, True, True)
-
-    def forward(k, d):
-        @pl.when(z >= d)
-        def _():
-            o = c - 2 * d
-            g_copy(k, o, 2).wait_recv()
-            pass_on(k, o, start, True, False)
-
-        @pl.when(z + d < n_z)
-        def _():
-            o = c + 2 * d
-            g_copy(k, o, 2).wait_recv()
-            pass_on(k, o, start, False, True)
+        spread(k, start)
+
+    def forward(k, do, receive):
+        def step(side, d, o):
+            copy = along_y(k, side, d, o)
+            if receive:
+                copy.wait_recv()
+            do(copy)
+
+        for d in range(1, n_z):
+            pl.when(z + d < n_z)(lambda d=d: step(0, d, c + 2 * d))
+            pl.when(z >= d)(lambda d=d: step(1, d, c - 2 * d))
 
     def blocks_product(k, j):
         rows = pl.ds(k * deep, deep)
         cols = pl.ds(pl.multiple_of(j * width, width), width)
-        return dot(xq[k], sbuf[rows, cols].astype(jnp.bfloat16))
+        return dot(xq[k], sb[rows, cols])
 
     def inner(k):
         return lax.dot_general(
@@ -194,31 +219,30 @@
 
     def complete(k):
         for z0 in range(n_z):
-            g_copy(k, z0 * 2 + 1 - y, 2).wait_recv()
-        for i in range(k * S_COPIES // CHUNKS, (k + 1) * S_COPIES // CHUNKS):
-            s_copy(i).wait()
+            o = z0 * 2 + 1 - y
+            along_y(k, 0, 0, o).wait_recv()
+
+    def product(k):
+        @pl.loop(0, n_row)
+        def _(j):
+            if k == 0:
+                acc[j] = blocks_product(k, j)
+            else:
+                acc[j] += blocks_product(k, j)
 
     for k in range(CHUNKS):
         post(k)
-    others(n_dev, me, lambda d: e_copy(d, me).start())
-    ebuf[me] = xg[me]
-
     gram = None
-    for step in range(1, CHUNKS + n_z - 1):
-        for d in range(n_z - 1, 0, -1):
-            if 0 <= step - d < CHUNKS:
-                forward(step - d, d)
-        k = step - (n_z - 1)
-        if 0 <= k < CHUNKS - 1:
-            complete(k)
-            gram = inner(k) if gram is None else gram + inner(k)
-
-            @pl.loop(0, n_row)
-            def _(j, k=k):
-                if k == 0:
-                    acc[j] = blocks_product(k, j)
-                else:
-                    acc[j] += blocks_product(k, j)
+    for k in range(CHUNKS + 1):
+        if k < CHUNKS:
+            forward(k, start, True)
+        piece = S_COPIES // 2 + k
+        if piece < S_COPIES:
+            convert(piece)
+        if 1 <= k < CHUNKS:
+            complete(k - 1)
+            gram = inner(k - 1) if gram is None else gram + inner(k - 1)
+            product(k - 1)
 
     last = CHUNKS - 1
     complete(last)
@@ -293,10 +317,8 @@
     others(n_col, c, lambda p: ab_copy(p, c).wait_send())
     others(n_dev, me, lambda d: e_copy(d, me).wait_send())
     for k in range(CHUNKS):
-        pass_on(k, c, wait_send, True, True)
-        for d in range(1, n_z):
-            pl.when(z >= d)(lambda k=k, d=d: pass_on(k, c - 2 * d, wait_send, True, False))
-            pl.when(z + d < n_z)(lambda k=k, d=d: pass_on(k, c + 2 * d, wait_send, False, True))
+        spread(k, wait_send)
+        forward(k, wait_send, False)
     core_copy(0, cross).wait_send()
     core_copy(1, near).wait_send()
     x_copy.wait_send()
@@ -315,18 +337,30 @@
 
     def tiled(rows):
         shaped = rows.reshape(own, n_dev, groups, LANES)
-        return shaped.transpose(1, 2, 0, 3).reshape(n_dev, 1, TILE, LANES)
-
-    xg = jnp.concatenate([tiled(orbitals), tiled(gradient)], axis=1)
+        return shaped.transpose(1, 2, 0, 3).reshape(n_dev, TILE, LANES)
+
+    def gather_rows(blocks, rows):
+        perm = np.zeros((blocks * TILE, blocks * TILE), np.float32)
+        for at in range(blocks * TILE):
+            group, rest = divmod(at, blocks * rows)
+            block, row = divmod(rest, rows)
+            perm[at, block * TILE + group * rows + row] = 1.0
+        if perm.shape[1] > LANES:
+            perm = perm.reshape(perm.shape[0], -1, LANES).transpose(1, 0, 2)
+        return jnp.asarray(perm, jnp.bfloat16)
+
     bf16, f32 = jnp.bfloat16, jnp.float32
     dma = pltpu.SemaphoreType.DMA
     tiles = pl.pallas_call(
         functools.partial(kernel, n_row, n_col, own, width),
         out_shape=jax.ShapeDtypeStruct((n_dev, TILE, LANES), bf16),
-        in_specs=[pl.BlockSpec(memory_space=pltpu.VMEM), pl.BlockSpec(memory_space=pl.ANY)],
+        in_specs=[pl.BlockSpec(memory_space=pl.ANY)] * 5,
         out_specs=pl.BlockSpec(memory_space=pltpu.VMEM),
         scratch_shapes=[
-            pltpu.VMEM(stored.shape, f32),
+            pltpu.VMEM((n_dev, 2, TILE, LANES), bf16),
+            pltpu.VMEM((n_row * TILE, n_row * TILE), bf16),
+            pltpu.VMEM((S_SLOTS, stored.shape[0] // S_COPIES, stored.shape[1]), f32),
+            pltpu.VMEM(stored.shape, bf16),
             pltpu.VMEM((n_row, n_col, 2, TILE, LANES), bf16),
             pltpu.VMEM((CHUNKS, n_pw, deep), bf16),
             pltpu.VMEM((CHUNKS, 2 * tall, deep), bf16),
@@ -341,8 +375,8 @@
             pltpu.VMEM((n_row, 2 * tall, n_pw), f32),
             pltpu.VMEM((n_col, 2 * tall, n_pw), f32),
             pltpu.VMEM((n_dev, TILE, LANES), bf16),
-            dma((S_COPIES,)), dma((n_row,)), dma((n_row,)), dma((n_dev,)), dma((n_dev,)),
-            dma((CHUNKS, n_col, 3)), dma((CHUNKS, n_col)),
+            dma((3 + n_dev * TILE // LANES,)), dma((S_COPIES,)), dma((n_row,)), dma((n_row,)), dma((n_dev,)), dma((n_dev,)),
+            dma((CHUNKS, 2, n_col // 2, 2)), dma((CHUNKS, n_col)),
             dma((n_row,)), dma((n_row,)), dma((n_col,)), dma((n_col,)),
             dma((2,)), dma((2,)), dma(()), dma(()), dma((n_dev,)), dma((n_dev,)),
         ],
@@ -350,7 +384,7 @@
             collective_id=0, has_side_effects=True, vmem_limit_bytes=56 * 1024 * 1024),
         cost_estimate=pl.CostEstimate(
             flops=2 * n_pw * stored.size, bytes_accessed=4 * stored.size, transcendentals=0),
-    )(xg, stored)
+    )(tiled(orbitals), tiled(gradient), gather_rows(n_dev, own), gather_rows(n_row, own), stored)
     shaped = tiles.reshape(n_dev, groups, own, LANES)
     return shaped.transpose(2, 0, 1, 3).reshape(own, n_orb)
 

time: 62.3 us -> 53.5 us (0.86)
  Pallas kernels: 58.8 us -> 51.7 us
  other arithmetic: 1.68 us -> 0 us
    pallas_call x1, Pallas kernels: 58.8 us -> 51.7 us  [kernel_body(): pl.pallas_call(functools.partial(kernel, n_row, n_col, own, width), out_s...]
    concatenate x1 -> x0, other arithmetic: 1.68 us -> none  [kernel_body(): xg = jnp.concatenate([tiled(orbitals), tiled(gradient)], axis=1)]
where the time goes in v2:
time: 53.5 us; the launch traced here: 53.4 us
  Pallas kernels  51.7 us (97%)
  local copies, waits for them, and re-layouts  1.61 us (3%)
    pallas_call x1, Pallas kernels, kernel_body(): pl.pallas_call(functools.partial(kernel, n_row, n_col, own, width), out_s...  51.7 us
    unnamed x1, local copies, waits for them, and re-layouts  1.61 us

profile of v2, /device:TPU:0, one launch (start us, length us, event | category | flops | bytes accessed | tf_op | source)
XLA Modules:
  0.0 53.4 jit_solution(9875359362771851029)
XLA Ops:
  0.0 51.7 %shard_map.55 = bf16[32,16,128]{2,1,0:T(8,128)(2,1)} custom-call(bf16[32,16,128]{2,1,0:T(8,128)(2,1)} %bitcast.16, bf16[32,16,128]{2,1,0:T(8,128)(2,1)} %bitcast.17, bf16[4,512,128]{2,1,0:T(8,128)(2,1)} %constant.4.clone.perm_hbm, bf16[64,64]{1,0:T(8,128)(2,1)} %constant.5.clone.small_hbm, f32[4096,2048]{1,0:T(8,128)} %s_hbm.1), custom_call_target="tpu_custom_call" | custom-call | flops 2147483648 | bytes 33554432 | tf_op jit(solution)/shard_map/pallas_call | solution.py:354
  51.7 1.6 %copy.10 = bf16[4,16384]{1,0:T(4,128)(2,1)} copy(bf16[4,16384]{1,0:T(4,128)(2,1)} %bitcast.15) | data formatting | bytes 262144

commit v3 on v2

--- a/solution.py
+++ b/solution.py
@@ -65,9 +65,11 @@
 def kernel(
     n_row, n_col, own, width,
     x_hbm, g_hbm, perm_hbm, small_hbm, s_hbm, out,
-    xg, small, sbuf, sb, rowbuf, xq, gsh, acc, rbuf, xout, xbuf, ebuf, xe, ge, perm, cbuf, ab, fbuf,
-    in_sem, s_sem, row_send, row_recv, e_send, e_recv, g_send, g_recv,
-    c_send, c_recv, ab_send, ab_recv, core_send, core_recv, x_send, x_recv, f_send, f_recv,
+    xin, gin, small, sbuf, sb, xt, grow, gblk, gt, xq, gsh, acc, rbuf, xout, xbuf, xe, ge, perm,
+    cbuf, ab, fbuf, fmid,
+    in_sem, s_sem, row_send, row_recv, e_send, e_recv, g_send, g_recv, xe_send, xe_recv,
+    c_send, c_recv, ab_send, ab_recv, core_send, core_recv, x_send, x_recv,
+    f_send, f_recv, h_send, h_recv,
 ):
     n_dev = n_row * n_col
     n_z = n_col // 2
@@ -75,16 +77,13 @@
     part = n_col // CHUNKS
     deep = part * width
     r, c = lax.axis_index("row"), lax.axis_index("col")
-    me = c * n_row + r
+    per = n_col // n_row
     z, y = lax.div(c, 2), lax.rem(c, 2)
     core, chip = lax.rem(r, 2), lax.div(r, 2)
     near = chip * 2 + 1 - core
     far = (1 - chip) * 2 + core
     cross = (1 - chip) * 2 + 1 - core
 
-    def device(d):
-        return {"row": lax.rem(d, n_row), "col": lax.div(d, n_row)}
-
     def remote(src, dst, send, recv, target):
         return pltpu.make_async_remote_copy(
             src_ref=src, dst_ref=dst, send_sem=send, recv_sem=recv,
@@ -111,8 +110,8 @@
             s_copy(i + S_SLOTS).start()
 
     local = [
-        pltpu.make_async_copy(x_hbm, xg.at[:, 0], in_sem.at[0]),
-        pltpu.make_async_copy(g_hbm, xg.at[:, 1], in_sem.at[1]),
+        pltpu.make_async_copy(x_hbm, xin, in_sem.at[0]),
+        pltpu.make_async_copy(g_hbm, gin, in_sem.at[1]),
         pltpu.make_async_copy(small_hbm, small, in_sem.at[2]),
     ] + [
         pltpu.make_async_copy(
@@ -130,40 +129,51 @@
             body(lax.rem(mine + i, count))
 
     barrier = pltpu.get_barrier_semaphore()
-    others(n_dev, me, lambda d: pl.semaphore_signal(
-        barrier, inc=1, device_id=device(d), device_id_type=MESH))
+    others(n_row, r, lambda p: pl.semaphore_signal(
+        barrier, inc=1, device_id={"row": p, "col": c}, device_id_type=MESH))
+    others(n_col, c, lambda p: pl.semaphore_signal(
+        barrier, inc=1, device_id={"row": r, "col": p}, device_id_type=MESH))
     for copy in local:
         copy.wait()
-    pl.semaphore_wait(barrier, n_dev - 1)
-
-    def row_copy(p, q):
-        return remote(
-            xg.at[pl.ds(p * n_col, n_col)], rowbuf.at[q],
-            row_send.at[p], row_recv.at[q], {"row": p, "col": c},
+    pl.semaphore_wait(barrier, n_row + n_col - 2)
+
+    def x_row(p, q):
+        return remote(
+            xin.at[pl.ds(p * n_col, n_col)], xt.at[c, lax.div(q, 2), :, lax.rem(q, 2)],
+            row_send.at[0, p], row_recv.at[0, q], {"row": p, "col": c},
         )
 
-    others(n_row, r, lambda p: row_copy(p, r).start())
-    rowbuf[r] = xg[pl.ds(r * n_col, n_col)]
-
-    def e_copy(d, s):
-        return remote(xg.at[d], ebuf.at[s], e_send.at[d], e_recv.at[s], device(d))
-
-    others(n_dev, me, lambda d: e_copy(d, me).start())
-    ebuf[me] = xg[me]
+    def g_row(p, q):
+        return remote(
+            gin.at[pl.ds(p * per, per)], grow.at[q],
+            row_send.at[1, p], row_recv.at[1, q], {"row": p, "col": c},
+        )
+
+    def g_blocks(p, q):
+        return remote(
+            gin.at[:, p], gblk.at[q],
+            row_send.at[2, p], row_recv.at[2, q], {"row": p, "col": c},
+        )
+
+    for p in (near, far, cross):
+        x_row(p, r).start()
+    others(n_row, r, lambda p: g_blocks(p, r).start())
+    others(n_row, r, lambda p: g_row(p, r).start())
+    xt[c, chip, :, core] = xin[pl.ds(r * n_col, n_col)]
+    gblk[r] = gin[:, r]
+    grow[r] = gin[pl.ds(r * per, per)]
     n_out = n_dev * TILE
     wide = n_dev * own
     tall = n_row * own
-    for i in range(S_COPIES // 2):
-        convert(i)
-
-    others(n_row, r, lambda q: row_copy(q, q).wait_recv())
-
-    def shard(k, o):
-        return xq.at[k, pl.ds(pl.multiple_of(o * tall, tall), tall), :]
-
-    def g_copy(k, o, send, target):
-        return remote(
-            shard(k, o), shard(k, o), send, g_recv.at[k, o], {"row": r, "col": target})
+
+    def unit(u, o):
+        if u == 0:
+            return xt.at[o, chip]
+        return xt.at[o, 1 - chip, pl.ds((u - 1) * part, part)]
+
+    def g_copy(u, o, send, target):
+        return remote(
+            unit(u, o), unit(u, o), send, g_recv.at[u, o], {"row": r, "col": target})
 
     def along_z(k, side, d):
         return g_copy(k, c, g_send.at[k, side, d, 0], c + 2 * d if side == 0 else c - 2 * d)
@@ -182,20 +192,6 @@
 
     def wait_send(copy):
         copy.wait_send()
-
-    def post(k):
-        mine = pl.ds(pl.multiple_of(c * tall, tall), tall)
-        for b in range(part):
-            for t in range(2):
-                block = rowbuf[:, k * part + b, t].reshape(n_row * TILE, LANES)
-                turned = dot(small[...], block).astype(jnp.bfloat16)
-                for g in range(groups):
-                    piece = turned[g * tall:(g + 1) * tall]
-                    lanes = pl.ds(b * width + g * LANES, LANES)
-                    gsh[k, t * tall:(t + 1) * tall, lanes] = piece
-                    if t == 0:
-                        xq[k, mine, lanes] = piece
-        spread(k, start)
 
     def forward(k, do, receive):
         def step(side, d, o):
@@ -217,10 +213,27 @@
         return lax.dot_general(
             gsh[k], xq[k], (((1,), (1,)), ((), ())), preferred_element_type=jnp.float32)
 
-    def complete(k):
+    def complete(u):
         for z0 in range(n_z):
             o = z0 * 2 + 1 - y
-            along_y(k, 0, 0, o).wait_recv()
+            along_y(u, 0, 0, o).wait_recv()
+
+    def arrange(k):
+        complete(k + 1)
+        blocks = [xt[:, :, k * part + b].reshape(n_out, LANES) for b in range(part)]
+        turned = dot(perm[...], jnp.concatenate(blocks, axis=1)).astype(jnp.bfloat16)
+        for b in range(part):
+            for g in range(groups):
+                lanes = pl.ds(b * width + g * LANES, LANES)
+                xq[k, :, lanes] = turned[g * wide:(g + 1) * wide, b * LANES:(b + 1) * LANES]
+        gsh[k, :tall, :] = xq[k, pl.ds(pl.multiple_of(c * tall, tall), tall), :]
+        for b in range(part):
+            high, low = divmod(k * part + b, n_row)
+            block = grow[:, high, low].reshape(n_row * TILE, LANES)
+            turned = dot(small[...], block).astype(jnp.bfloat16)
+            for g in range(groups):
+                lanes = pl.ds(b * width + g * LANES, LANES)
+                gsh[k, tall:, lanes] = turned[g * tall:(g + 1) * tall]
 
     def product(k):
         @pl.loop(0, n_row)
@@ -230,22 +243,53 @@
             else:
                 acc[j] += blocks_product(k, j)
 
+    def e_copy(p, q):
+        return remote(gblk.at[:, p], gt.at[q], e_send.at[p], e_recv.at[q], {"row": r, "col": p})
+
+    x_row(near, near).wait_recv()
+    spread(0, start)
+    convert(0)
+    convert(1)
+    x_row(far, far).wait_recv()
+    x_row(cross, cross).wait_recv()
     for k in range(CHUNKS):
-        post(k)
+        spread(k + 1, start)
+    others(n_row, r, lambda q: g_blocks(q, q).wait_recv())
+    others(n_col, c, lambda p: e_copy(p, c).start())
+    gt[c] = gblk[:, c]
+    forward(0, start, True)
+    convert(2)
+    convert(3)
+    others(n_row, r, lambda q: g_row(q, q).wait_recv())
     gram = None
-    for k in range(CHUNKS + 1):
-        if k < CHUNKS:
-            forward(k, start, True)
-        piece = S_COPIES // 2 + k
-        if piece < S_COPIES:
-            convert(piece)
-        if 1 <= k < CHUNKS:
-            complete(k - 1)
+    for k in range(CHUNKS):
+        forward(k + 1, start, True)
+        convert(S_COPIES // 2 + k)
+        if k == 0:
+            complete(0)
+        else:
+            arrange(k - 1)
             gram = inner(k - 1) if gram is None else gram + inner(k - 1)
             product(k - 1)
 
     last = CHUNKS - 1
-    complete(last)
+    arrange(last)
+    holder = lax.div(c, per)
+
+    def xe_copy(p):
+        block = lax.rem(c, per) * n_row + p
+        lanes = pl.ds(pl.multiple_of(lax.rem(block, part) * width, width), width)
+        return remote(
+            xq.at[lax.div(block, part), :, lanes], xe,
+            xe_send.at[p], xe_recv, {"row": p, "col": c})
+
+    @pl.when(r == holder)
+    def _():
+        others(n_row, r, lambda p: xe_copy(p).start())
+        block = lax.rem(c, per) * n_row + r
+        lanes = pl.ds(pl.multiple_of(lax.rem(block, part) * width, width), width)
+        xe[...] = xq[lax.div(block, part), :, lanes]
+
     cbuf[r] = gram + inner(last)
 
     def c_copy(p, q):
@@ -280,11 +324,11 @@
     x_copy.start()
     acc[r] += blocks_product(last, r)
 
-    others(n_dev, me, lambda s: e_copy(s, s).wait_recv())
-    for t, dest in ((0, xe), (1, ge)):
-        turned = dot(perm[...], ebuf[:, t].reshape(n_out, LANES)).astype(jnp.bfloat16)
-        for g in range(groups):
-            dest[:, g * LANES:(g + 1) * LANES] = turned[g * wide:(g + 1) * wide]
+    others(n_col, c, lambda q: e_copy(q, q).wait_recv())
+    turned = dot(perm[...], gt[...].reshape(n_out, LANES)).astype(jnp.bfloat16)
+    for g in range(groups):
+        ge[:, g * LANES:(g + 1) * LANES] = turned[g * wide:(g + 1) * wide]
+    pl.when(r != holder)(lambda: xe_copy(r).wait_recv())
 
     others(n_col, c, lambda q: ab_copy(q, q).wait_recv())
     orb_orb = ab[:, :tall, :].reshape(wide, wide)
@@ -304,26 +348,40 @@
     stack = jnp.concatenate([result[:, g * LANES:(g + 1) * LANES] for g in range(groups)], axis=0)
     tiles = lax.dot_general(
         perm[...], stack, (((0,), (0,)), ((), ())), preferred_element_type=jnp.float32)
-    fbuf[...] = tiles.astype(jnp.bfloat16).reshape(n_dev, TILE, LANES)
-
-    def f_copy(d, s):
-        return remote(fbuf.at[d], out.at[s], f_send.at[d], f_recv.at[s], device(d))
-
-    others(n_dev, me, lambda d: f_copy(d, me).start())
-    out[me] = fbuf[me]
-
-    others(n_row, r, lambda p: row_copy(p, r).wait_send())
+    fbuf[...] = tiles.astype(jnp.bfloat16).reshape(n_col, n_row, TILE, LANES)
+
+    def f_copy(p, q):
+        return remote(fbuf.at[p], fmid.at[q], f_send.at[p], f_recv.at[q], {"row": r, "col": p})
+
+    def h_copy(p, q):
+        return remote(
+            fmid.at[:, p], out.at[:, q], h_send.at[p], h_recv.at[q], {"row": p, "col": c})
+
+    others(n_col, c, lambda p: f_copy(p, c).start())
+    fmid[c] = fbuf[c]
+    others(n_col, c, lambda q: f_copy(q, q).wait_recv())
+    others(n_row, r, lambda p: h_copy(p, r).start())
+    out[:, r] = fmid[:, r]
+
+    for sent in (x_row, g_row, g_blocks):
+        others(n_row, r, lambda p, sent=sent: sent(p, r).wait_send())
+
+    @pl.when(r == holder)
+    def _():
+        others(n_row, r, lambda p: xe_copy(p).wait_send())
+
     others(n_row, r, lambda p: c_copy(p, r).wait_send())
     others(n_col, c, lambda p: ab_copy(p, c).wait_send())
-    others(n_dev, me, lambda d: e_copy(d, me).wait_send())
-    for k in range(CHUNKS):
+    others(n_col, c, lambda p: e_copy(p, c).wait_send())
+    for k in range(CHUNKS + 1):
         spread(k, wait_send)
         forward(k, wait_send, False)
     core_copy(0, cross).wait_send()
     core_copy(1, near).wait_send()
     x_copy.wait_send()
-    others(n_dev, me, lambda s: f_copy(s, s).wait_recv())
-    others(n_dev, me, lambda d: f_copy(d, me).wait_send())
+    others(n_col, c, lambda p: f_copy(p, c).wait_send())
+    others(n_row, r, lambda q: h_copy(q, q).wait_recv())
+    others(n_row, r, lambda p: h_copy(p, r).wait_send())
 
 
 def kernel_body(n_row, n_col, orbitals, gradient, stored):
@@ -353,38 +411,44 @@
     dma = pltpu.SemaphoreType.DMA
     tiles = pl.pallas_call(
         functools.partial(kernel, n_row, n_col, own, width),
-        out_shape=jax.ShapeDtypeStruct((n_dev, TILE, LANES), bf16),
+        out_shape=jax.ShapeDtypeStruct((n_col, n_row, TILE, LANES), bf16),
         in_specs=[pl.BlockSpec(memory_space=pl.ANY)] * 5,
         out_specs=pl.BlockSpec(memory_space=pltpu.VMEM),
         scratch_shapes=[
-            pltpu.VMEM((n_dev, 2, TILE, LANES), bf16),
+            pltpu.VMEM((n_dev, TILE, LANES), bf16),
+            pltpu.VMEM((n_col, n_row, TILE, LANES), bf16),
             pltpu.VMEM((n_row * TILE, n_row * TILE), bf16),
             pltpu.VMEM((S_SLOTS, stored.shape[0] // S_COPIES, stored.shape[1]), f32),
             pltpu.VMEM(stored.shape, bf16),
-            pltpu.VMEM((n_row, n_col, 2, TILE, LANES), bf16),
+            pltpu.VMEM((n_col, 2, n_col, 2, TILE, LANES), bf16),
+            pltpu.VMEM((n_row, n_col // n_row, n_row, TILE, LANES), bf16),
+            pltpu.VMEM((n_row, n_col, TILE, LANES), bf16),
+            pltpu.VMEM((n_col, n_row, TILE, LANES), bf16),
             pltpu.VMEM((CHUNKS, n_pw, deep), bf16),
             pltpu.VMEM((CHUNKS, 2 * tall, deep), bf16),
             pltpu.VMEM((n_row, n_pw, width), f32),
             pltpu.VMEM((2, n_pw, width), f32),
             pltpu.VMEM((n_pw, width), bf16),
             pltpu.VMEM((n_pw, width), bf16),
-            pltpu.VMEM((n_dev, 2, TILE, LANES), bf16),
             pltpu.VMEM((n_pw, width), bf16),
             pltpu.VMEM((n_pw, width), bf16),
             pltpu.VMEM((n_dev * TILE, n_dev * TILE), bf16),
             pltpu.VMEM((n_row, 2 * tall, n_pw), f32),
             pltpu.VMEM((n_col, 2 * tall, n_pw), f32),
-            pltpu.VMEM((n_dev, TILE, LANES), bf16),
-            dma((3 + n_dev * TILE // LANES,)), dma((S_COPIES,)), dma((n_row,)), dma((n_row,)), dma((n_dev,)), dma((n_dev,)),
-            dma((CHUNKS, 2, n_col // 2, 2)), dma((CHUNKS, n_col)),
+            pltpu.VMEM((n_col, n_row, TILE, LANES), bf16),
+            pltpu.VMEM((n_col, n_row, TILE, LANES), bf16),
+            dma((3 + n_dev * TILE // LANES,)), dma((S_COPIES,)), dma((3, n_row)), dma((3, n_row)),
+            dma((n_col,)), dma((n_col,)),
+            dma((CHUNKS + 1, 2, n_col // 2, 2)), dma((CHUNKS + 1, n_col)), dma((n_row,)), dma(()),
             dma((n_row,)), dma((n_row,)), dma((n_col,)), dma((n_col,)),
-            dma((2,)), dma((2,)), dma(()), dma(()), dma((n_dev,)), dma((n_dev,)),
+            dma((2,)), dma((2,)), dma(()), dma(()),
+            dma((n_col,)), dma((n_col,)), dma((n_row,)), dma((n_row,)),
         ],
         compiler_params=pltpu.CompilerParams(
             collective_id=0, has_side_effects=True, vmem_limit_bytes=56 * 1024 * 1024),
         cost_estimate=pl.CostEstimate(
             flops=2 * n_pw * stored.size, bytes_accessed=4 * stored.size, transcendentals=0),
-    )(tiled(orbitals), tiled(gradient), gather_rows(n_dev, own), gather_rows(n_row, own), stored)
+    )(tiled(orbitals), tiled(gradient).reshape(n_col, n_row, TILE, LANES), gather_rows(n_dev, own), gather_rows(n_row, own), stored)
     shaped = tiles.reshape(n_dev, groups, own, LANES)
     return shaped.transpose(2, 0, 1, 3).reshape(own, n_orb)
 
@@ -396,7 +460,7 @@
     n_dev = n_row * n_col
     width = n_orb // n_dev
     fits = (
-        n_row == 4 and n_col % CHUNKS == 0 and width % LANES == 0
+        n_row == 4 and n_col % CHUNKS == 0 and n_col % n_row == 0 and width % LANES == 0
         and own * width == TILE * LANES and own * n_row == TILE
         and own * n_dev == LANES and stored.shape[0] % S_COPIES == 0
         and stored.size * 4 <= 32 * 1024 * 1024

time: 53.5 us -> 57.8 us (1.080)
  Pallas kernels: 51.7 us -> 56 us
    pallas_call x1, Pallas kernels: 51.7 us -> 56 us  [kernel_body(): pl.pallas_call(functools.partial(kernel, n_row, n_col, own, width), out_s...]
where the time goes in v3:
time: 57.8 us; the launch traced here: 57.6 us
  Pallas kernels  56 us (97%)
  local copies, waits for them, and re-layouts  1.61 us (3%)
    pallas_call x1, Pallas kernels, kernel_body(): pl.pallas_call(functools.partial(kernel, n_row, n_col, own, width), out_s...  56 us
    unnamed x1, local copies, waits for them, and re-layouts  1.61 us

profile of v3, /device:TPU:0, one launch (start us, length us, event | category | flops | bytes accessed | tf_op | source)
XLA Modules:
  0.0 57.6 jit_solution(4733469556314481799)
XLA Ops:
  0.0 56.0 %shard_map.55 = bf16[8,4,16,128]{3,2,1,0:T(8,128)(2,1)} custom-call(bf16[32,16,128]{2,1,0:T(8,128)(2,1)} %bitcast.16, bf16[8,4,16,128]{3,2,1,0:T(8,128)(2,1)} %bitcast.17, bf16[4,512,128]{2,1,0:T(8,128)(2,1)} %constant.4.clone.perm_hbm, bf16[64,64]{1,0:T(8,128)(2,1)} %constant.5.clone.small_hbm, f32[4096,2048]{1,0:T(8,128)} %s_hbm.1), custom_call_target="tpu_custom_call" | custom-call | flops 2147483648 | bytes 33554432 | tf_op jit(solution)/shard_map/pallas_call | solution.py:412
  56.0 1.6 %copy.10 = bf16[4,16384]{1,0:T(4,128)(2,1)} copy(bf16[4,16384]{1,0:T(4,128)(2,1)} %bitcast.15) | data formatting | bytes 262144

commit v4 on v2

--- a/solution.py
+++ b/solution.py
@@ -165,17 +165,24 @@
         return remote(
             shard(k, o), shard(k, o), send, g_recv.at[k, o], {"row": r, "col": target})
 
+    up, down = n_z // 2, n_z - 1 - n_z // 2
+
     def along_z(k, side, d):
         return g_copy(k, c, g_send.at[k, side, d, 0], c + 2 * d if side == 0 else c - 2 * d)
 
     def along_y(k, side, d, o):
         return g_copy(k, o, g_send.at[k, side, d, 1], z * 2 + 1 - y)
+
+    def relay(k, side, d, o, t):
+        return g_copy(k, o, g_send.at[k, side, d, 2 + t], 2 * t + y)
 
     def spread(k, do):
         do(along_y(k, 0, 0, c))
         for d in range(1, n_z):
-            pl.when(z + d < n_z)(lambda d=d: do(along_z(k, 0, d)))
-            pl.when(z >= d)(lambda d=d: do(along_z(k, 1, d)))
+            to = z + d
+            pl.when((to < n_z) & ((z >= up) | (to <= up)))(lambda d=d: do(along_z(k, 0, d)))
+            to = z - d
+            pl.when((to >= 0) & ((z <= down) | (to >= down)))(lambda d=d: do(along_z(k, 1, d)))
 
     def start(copy):
         copy.start()
@@ -202,6 +209,16 @@
             copy = along_y(k, side, d, o)
             if receive:
                 copy.wait_recv()
+            if side == 0:
+                turn, targets = down, range(down)
+            else:
+                turn, targets = up, range(up + 1, n_z)
+
+            @pl.when(z == turn)
+            def _():
+                for t in targets:
+                    do(relay(k, side, d, o, t))
+
             do(copy)
 
         for d in range(1, n_z):
@@ -376,7 +393,7 @@
             pltpu.VMEM((n_col, 2 * tall, n_pw), f32),
             pltpu.VMEM((n_dev, TILE, LANES), bf16),
             dma((3 + n_dev * TILE // LANES,)), dma((S_COPIES,)), dma((n_row,)), dma((n_row,)), dma((n_dev,)), dma((n_dev,)),
-            dma((CHUNKS, 2, n_col // 2, 2)), dma((CHUNKS, n_col)),
+            dma((CHUNKS, 2, n_col // 2, 2 + n_col // 2)), dma((CHUNKS, n_col)),
             dma((n_row,)), dma((n_row,)), dma((n_col,)), dma((n_col,)),
             dma((2,)), dma((2,)), dma(()), dma(()), dma((n_dev,)), dma((n_dev,)),
         ],

time: 53.5 us -> 54.2 us (1.013)
  Pallas kernels: 51.7 us -> 52.5 us
    pallas_call x1, Pallas kernels: 51.7 us -> 52.5 us  [kernel_body(): pl.pallas_call(functools.partial(kernel, n_row, n_col, own, width), out_s...]
where the time goes in v4:
time: 54.2 us; the launch traced here: 54.1 us
  Pallas kernels  52.5 us (97%)
  local copies, waits for them, and re-layouts  1.61 us (3%)
    pallas_call x1, Pallas kernels, kernel_body(): pl.pallas_call(functools.partial(kernel, n_row, n_col, own, width), out_s...  52.5 us
    unnamed x1, local copies, waits for them, and re-layouts  1.61 us

profile of v4, /device:TPU:0, one launch (start us, length us, event | category | flops | bytes accessed | tf_op | source)
XLA Modules:
  0.0 54.1 jit_solution(16132974920657842642)
XLA Ops:
  0.0 52.5 %shard_map.55 = bf16[32,16,128]{2,1,0:T(8,128)(2,1)} custom-call(bf16[32,16,128]{2,1,0:T(8,128)(2,1)} %bitcast.16, bf16[32,16,128]{2,1,0:T(8,128)(2,1)} %bitcast.17, bf16[4,512,128]{2,1,0:T(8,128)(2,1)} %constant.4.clone.perm_hbm, bf16[64,64]{1,0:T(8,128)(2,1)} %constant.5.clone.small_hbm, f32[4096,2048]{1,0:T(8,128)} %s_hbm.1), custom_call_target="tpu_custom_call" | custom-call | flops 2147483648 | bytes 33554432 | tf_op jit(solution)/shard_map/pallas_call | solution.py:371
  52.5 1.6 %copy.10 = bf16[4,16384]{1,0:T(4,128)(2,1)} copy(bf16[4,16384]{1,0:T(4,128)(2,1)} %bitcast.15) | data formatting | bytes 262144

commit v5 on v2

--- a/solution.py
+++ b/solution.py
@@ -64,8 +64,8 @@
 
 def kernel(
     n_row, n_col, own, width,
-    x_hbm, g_hbm, perm_hbm, small_hbm, s_hbm, out,
-    xg, small, sbuf, sb, rowbuf, xq, gsh, acc, rbuf, xout, xbuf, ebuf, xe, ge, perm, cbuf, ab, fbuf,
+    x_hbm, g_hbm, perm_hbm, back_hbm, small_hbm, s_hbm, out,
+    xg, small, sbuf, sb, rowbuf, xq, gsh, acc, rbuf, xout, xbuf, ebuf, xe, ge, perm, back, cbuf, ab, fbuf,
     in_sem, s_sem, row_send, row_recv, e_send, e_recv, g_send, g_recv,
     c_send, c_recv, ab_send, ab_recv, core_send, core_recv, x_send, x_recv, f_send, f_recv,
 ):
@@ -118,6 +118,11 @@
         pltpu.make_async_copy(
             perm_hbm.at[g], perm.at[:, pl.ds(g * LANES, LANES)], in_sem.at[3 + g])
         for g in range(perm_hbm.shape[0])
+    ] + [
+        pltpu.make_async_copy(
+            back_hbm.at[g], back.at[:, pl.ds(g * LANES, LANES)],
+            in_sem.at[3 + perm_hbm.shape[0] + g])
+        for g in range(perm_hbm.shape[0])
     ]
     for copy in local:
         copy.start()
@@ -153,9 +158,6 @@
     n_out = n_dev * TILE
     wide = n_dev * own
     tall = n_row * own
-    for i in range(S_COPIES // 2):
-        convert(i)
-
     others(n_row, r, lambda q: row_copy(q, q).wait_recv())
 
     def shard(k, o):
@@ -232,17 +234,21 @@
 
     for k in range(CHUNKS):
         post(k)
+    forward(0, start, True)
     gram = None
-    for k in range(CHUNKS + 1):
-        if k < CHUNKS:
-            forward(k, start, True)
-        piece = S_COPIES // 2 + k
-        if piece < S_COPIES:
-            convert(piece)
-        if 1 <= k < CHUNKS:
-            complete(k - 1)
-            gram = inner(k - 1) if gram is None else gram + inner(k - 1)
-            product(k - 1)
+    pieces = iter(range(S_COPIES))
+    for k in range(CHUNKS - 1):
+        for _ in range(2):
+            convert(next(pieces))
+        forward(k + 1, start, True)
+        if k > 0:
+            convert(next(pieces))
+        if k == CHUNKS - 2:
+            for piece in pieces:
+                convert(piece)
+        complete(k)
+        gram = inner(k) if gram is None else gram + inner(k)
+        product(k)
 
     last = CHUNKS - 1
     complete(last)
@@ -302,8 +308,7 @@
     x_copy.wait_recv()
     result = (rest - xbuf[...].astype(jnp.float32)).astype(jnp.bfloat16)
     stack = jnp.concatenate([result[:, g * LANES:(g + 1) * LANES] for g in range(groups)], axis=0)
-    tiles = lax.dot_general(
-        perm[...], stack, (((0,), (0,)), ((), ())), preferred_element_type=jnp.float32)
+    tiles = dot(back[...], stack)
     fbuf[...] = tiles.astype(jnp.bfloat16).reshape(n_dev, TILE, LANES)
 
     def f_copy(d, s):
@@ -345,16 +350,19 @@
             group, rest = divmod(at, blocks * rows)
             block, row = divmod(rest, rows)
             perm[at, block * TILE + group * rows + row] = 1.0
-        if perm.shape[1] > LANES:
-            perm = perm.reshape(perm.shape[0], -1, LANES).transpose(1, 0, 2)
-        return jnp.asarray(perm, jnp.bfloat16)
-
+        return perm
+
+    def by_lanes(perm):
+        return jnp.asarray(perm.reshape(perm.shape[0], -1, LANES).transpose(1, 0, 2), jnp.bfloat16)
+
+    perm = gather_rows(n_dev, own)
+    small = jnp.asarray(gather_rows(n_row, own), jnp.bfloat16)
     bf16, f32 = jnp.bfloat16, jnp.float32
     dma = pltpu.SemaphoreType.DMA
     tiles = pl.pallas_call(
         functools.partial(kernel, n_row, n_col, own, width),
         out_shape=jax.ShapeDtypeStruct((n_dev, TILE, LANES), bf16),
-        in_specs=[pl.BlockSpec(memory_space=pl.ANY)] * 5,
+        in_specs=[pl.BlockSpec(memory_space=pl.ANY)] * 6,
         out_specs=pl.BlockSpec(memory_space=pltpu.VMEM),
         scratch_shapes=[
             pltpu.VMEM((n_dev, 2, TILE, LANES), bf16),
@@ -372,10 +380,11 @@
             pltpu.VMEM((n_pw, width), bf16),
             pltpu.VMEM((n_pw, width), bf16),
             pltpu.VMEM((n_dev * TILE, n_dev * TILE), bf16),
+            pltpu.VMEM((n_dev * TILE, n_dev * TILE), bf16),
             pltpu.VMEM((n_row, 2 * tall, n_pw), f32),
             pltpu.VMEM((n_col, 2 * tall, n_pw), f32),
             pltpu.VMEM((n_dev, TILE, LANES), bf16),
-            dma((3 + n_dev * TILE // LANES,)), dma((S_COPIES,)), dma((n_row,)), dma((n_row,)), dma((n_dev,)), dma((n_dev,)),
+            dma((3 + 2 * n_dev * TILE // LANES,)), dma((S_COPIES,)), dma((n_row,)), dma((n_row,)), dma((n_dev,)), dma((n_dev,)),
             dma((CHUNKS, 2, n_col // 2, 2)), dma((CHUNKS, n_col)),
             dma((n_row,)), dma((n_row,)), dma((n_col,)), dma((n_col,)),
             dma((2,)), dma((2,)), dma(()), dma(()), dma((n_dev,)), dma((n_dev,)),
@@ -384,7 +393,7 @@
             collective_id=0, has_side_effects=True, vmem_limit_bytes=56 * 1024 * 1024),
         cost_estimate=pl.CostEstimate(
             flops=2 * n_pw * stored.size, bytes_accessed=4 * stored.size, transcendentals=0),
-    )(tiled(orbitals), tiled(gradient), gather_rows(n_dev, own), gather_rows(n_row, own), stored)
+    )(tiled(orbitals), tiled(gradient), by_lanes(perm), by_lanes(perm.T), small, stored)
     shaped = tiles.reshape(n_dev, groups, own, LANES)
     return shaped.transpose(2, 0, 1, 3).reshape(own, n_orb)
 

time: 53.5 us -> 54.6 us (1.021)
  Pallas kernels: 51.7 us -> 52.9 us
    pallas_call x1, Pallas kernels: 51.7 us -> 52.9 us  [kernel_body(): pl.pallas_call(functools.partial(kernel, n_row, n_col, own, width), out_s...]
where the time goes in v5:
time: 54.6 us; the launch traced here: 54.5 us
  Pallas kernels  52.9 us (97%)
  local copies, waits for them, and re-layouts  1.61 us (3%)
    pallas_call x1, Pallas kernels, kernel_body(): pl.pallas_call(functools.partial(kernel, n_row, n_col, own, width), out_s...  52.9 us
    unnamed x1, local copies, waits for them, and re-layouts  1.61 us

profile of v5, /device:TPU:0, one launch (start us, length us, event | category | flops | bytes accessed | tf_op | source)
XLA Modules:
  0.0 54.5 jit_solution(11115955423450180982)
XLA Ops:
  0.0 52.9 %shard_map.64 = bf16[32,16,128]{2,1,0:T(8,128)(2,1)} custom-call(bf16[32,16,128]{2,1,0:T(8,128)(2,1)} %bitcast.16, bf16[32,16,128]{2,1,0:T(8,128)(2,1)} %bitcast.17, bf16[4,512,128]{2,1,0:T(8,128)(2,1)} %constant.7.clone.perm_hbm, bf16[4,512,128]{2,1,0:T(8,128)(2,1)} %constant.8.clone.back_hbm, bf16[64,64]{1,0:T(8,128)(2,1)} %constant.6.clone.small_hbm, ...), custom_call_target="tpu_custom_call" | custom-call | flops 2147483648 | bytes 33554432 | tf_op jit(solution)/shard_map/pallas_call | solution.py:362
  52.9 1.6 %copy.11 = bf16[4,16384]{1,0:T(4,128)(2,1)} copy(bf16[4,16384]{1,0:T(4,128)(2,1)} %bitcast.15) | data formatting | bytes 262144

commit v6 on v5

--- a/solution.py
+++ b/solution.py
@@ -151,10 +151,10 @@
     rowbuf[r] = xg[pl.ds(r * n_col, n_col)]
 
     def e_copy(d, s):
-        return remote(xg.at[d], ebuf.at[s], e_send.at[d], e_recv.at[s], device(d))
-
-    others(n_dev, me, lambda d: e_copy(d, me).start())
-    ebuf[me] = xg[me]
+        return remote(xg.at[d], ebuf.at[s], e_send, e_recv, device(d))
+
+    for i in range(S_COPIES // 2):
+        convert(i)
     n_out = n_dev * TILE
     wide = n_dev * own
     tall = n_row * own
@@ -234,21 +234,20 @@
 
     for k in range(CHUNKS):
         post(k)
-    forward(0, start, True)
     gram = None
-    pieces = iter(range(S_COPIES))
-    for k in range(CHUNKS - 1):
-        for _ in range(2):
-            convert(next(pieces))
-        forward(k + 1, start, True)
-        if k > 0:
-            convert(next(pieces))
-        if k == CHUNKS - 2:
-            for piece in pieces:
-                convert(piece)
-        complete(k)
-        gram = inner(k) if gram is None else gram + inner(k)
-        product(k)
+    for k in range(CHUNKS + 1):
+        if k < CHUNKS:
+            forward(k, start, True)
+        if k == CHUNKS - 1:
+            others(n_dev, me, lambda d: e_copy(d, me).start())
+            ebuf[me] = xg[me]
+        piece = S_COPIES // 2 + k
+        if piece < S_COPIES:
+            convert(piece)
+        if 1 <= k < CHUNKS:
+            complete(k - 1)
+            gram = inner(k - 1) if gram is None else gram + inner(k - 1)
+            product(k - 1)
 
     last = CHUNKS - 1
     complete(last)
@@ -286,7 +285,9 @@
     x_copy.start()
     acc[r] += blocks_product(last, r)
 
-    others(n_dev, me, lambda s: e_copy(s, s).wait_recv())
+    rest_of = pl.ds(0, n_dev - 1)
+    e_all = remote(xg.at[rest_of], ebuf.at[rest_of], e_send, e_recv, device(me))
+    e_all.wait_recv()
     for t, dest in ((0, xe), (1, ge)):
         turned = dot(perm[...], ebuf[:, t].reshape(n_out, LANES)).astype(jnp.bfloat16)
         for g in range(groups):
@@ -312,7 +313,7 @@
     fbuf[...] = tiles.astype(jnp.bfloat16).reshape(n_dev, TILE, LANES)
 
     def f_copy(d, s):
-        return remote(fbuf.at[d], out.at[s], f_send.at[d], f_recv.at[s], device(d))
+        return remote(fbuf.at[d], out.at[s], f_send, f_recv, device(d))
 
     others(n_dev, me, lambda d: f_copy(d, me).start())
     out[me] = fbuf[me]
@@ -320,15 +321,16 @@
     others(n_row, r, lambda p: row_copy(p, r).wait_send())
     others(n_row, r, lambda p: c_copy(p, r).wait_send())
     others(n_col, c, lambda p: ab_copy(p, c).wait_send())
-    others(n_dev, me, lambda d: e_copy(d, me).wait_send())
+    e_all.wait_send()
     for k in range(CHUNKS):
         spread(k, wait_send)
         forward(k, wait_send, False)
     core_copy(0, cross).wait_send()
     core_copy(1, near).wait_send()
     x_copy.wait_send()
-    others(n_dev, me, lambda s: f_copy(s, s).wait_recv())
-    others(n_dev, me, lambda d: f_copy(d, me).wait_send())
+    f_all = remote(fbuf.at[rest_of], out.at[rest_of], f_send, f_recv, device(me))
+    f_all.wait_recv()
+    f_all.wait_send()
 
 
 def kernel_body(n_row, n_col, orbitals, gradient, stored):
@@ -384,10 +386,10 @@
             pltpu.VMEM((n_row, 2 * tall, n_pw), f32),
             pltpu.VMEM((n_col, 2 * tall, n_pw), f32),
             pltpu.VMEM((n_dev, TILE, LANES), bf16),
-            dma((3 + 2 * n_dev * TILE // LANES,)), dma((S_COPIES,)), dma((n_row,)), dma((n_row,)), dma((n_dev,)), dma((n_dev,)),
+            dma((3 + 2 * n_dev * TILE // LANES,)), dma((S_COPIES,)), dma((n_row,)), dma((n_row,)), dma(()), dma(()),
             dma((CHUNKS, 2, n_col // 2, 2)), dma((CHUNKS, n_col)),
             dma((n_row,)), dma((n_row,)), dma((n_col,)), dma((n_col,)),
-            dma((2,)), dma((2,)), dma(()), dma(()), dma((n_dev,)), dma((n_dev,)),
+            dma((2,)), dma((2,)), dma(()), dma(()), dma(()), dma(()),
         ],
         compiler_params=pltpu.CompilerParams(
             collective_id=0, has_side_effects=True, vmem_limit_bytes=56 * 1024 * 1024),

time: 54.6 us -> 53.1 us (0.973)
  Pallas kernels: 52.9 us -> 51.4 us
    pallas_call x1, Pallas kernels: 52.9 us -> 51.4 us  [kernel_body(): pl.pallas_call(functools.partial(kernel, n_row, n_col, own, width), out_s...]
where the time goes in v6:
time: 53.1 us; the launch traced here: 53 us
  Pallas kernels  51.4 us (97%)
  local copies, waits for them, and re-layouts  1.61 us (3%)
    pallas_call x1, Pallas kernels, kernel_body(): pl.pallas_call(functools.partial(kernel, n_row, n_col, own, width), out_s...  51.4 us
    unnamed x1, local copies, waits for them, and re-layouts  1.61 us

profile of v6, /device:TPU:0, one launch (start us, length us, event | category | flops | bytes accessed | tf_op | source)
XLA Modules:
  0.0 53.0 jit_solution(10852688983411849604)
XLA Ops:
  0.0 51.4 %shard_map.64 = bf16[32,16,128]{2,1,0:T(8,128)(2,1)} custom-call(bf16[32,16,128]{2,1,0:T(8,128)(2,1)} %bitcast.16, bf16[32,16,128]{2,1,0:T(8,128)(2,1)} %bitcast.17, bf16[4,512,128]{2,1,0:T(8,128)(2,1)} %constant.7.clone.perm_hbm, bf16[4,512,128]{2,1,0:T(8,128)(2,1)} %constant.8.clone.back_hbm, bf16[64,64]{1,0:T(8,128)(2,1)} %constant.6.clone.small_hbm, ...), custom_call_target="tpu_custom_call" | custom-call | flops 2147483648 | bytes 33554432 | tf_op jit(solution)/shard_map/pallas_call | solution.py:364
  51.4 1.6 %copy.11 = bf16[4,16384]{1,0:T(4,128)(2,1)} copy(bf16[4,16384]{1,0:T(4,128)(2,1)} %bitcast.15) | data formatting | bytes 262144

commit v7 on v6

--- a/solution.py
+++ b/solution.py
@@ -11,7 +11,7 @@
 MESH = pl.DeviceIdType.MESH
 LANES = 128
 TILE = 16
-CHUNKS = 4
+CHUNKS = 8
 S_COPIES = 8
 S_SLOTS = 6
 

time: 53.1 us -> 55.8 us (1.051)
  Pallas kernels: 51.4 us -> 54 us
    pallas_call x1, Pallas kernels: 51.4 us -> 54 us  [kernel_body(): pl.pallas_call(functools.partial(kernel, n_row, n_col, own, width), out_s...]
where the time goes in v7:
time: 55.8 us; the launch traced here: 55.6 us
  Pallas kernels  54 us (97%)
  local copies, waits for them, and re-layouts  1.61 us (3%)
    pallas_call x1, Pallas kernels, kernel_body(): pl.pallas_call(functools.partial(kernel, n_row, n_col, own, width), out_s...  54 us
    unnamed x1, local copies, waits for them, and re-layouts  1.61 us

profile of v7, /device:TPU:0, one launch (start us, length us, event | category | flops | bytes accessed | tf_op | source)
XLA Modules:
  0.0 55.6 jit_solution(7050952863496578602)
XLA Ops:
  0.0 54.0 %shard_map.64 = bf16[32,16,128]{2,1,0:T(8,128)(2,1)} custom-call(bf16[32,16,128]{2,1,0:T(8,128)(2,1)} %bitcast.16, bf16[32,16,128]{2,1,0:T(8,128)(2,1)} %bitcast.17, bf16[4,512,128]{2,1,0:T(8,128)(2,1)} %constant.7.clone.perm_hbm, bf16[4,512,128]{2,1,0:T(8,128)(2,1)} %constant.8.clone.back_hbm, bf16[64,64]{1,0:T(8,128)(2,1)} %constant.6.clone.small_hbm, ...), custom_call_target="tpu_custom_call" | custom-call | flops 2147483648 | bytes 33554432 | tf_op jit(solution)/shard_map/pallas_call | solution.py:364
  54.0 1.6 %copy.11 = bf16[4,16384]{1,0:T(4,128)(2,1)} copy(bf16[4,16384]{1,0:T(4,128)(2,1)} %bitcast.15) | data formatting | bytes 262144
